TPU v7x, 256 devices: a whole 4x4x8 slice. The times are simulated.
256 devices in a mesh: fsdp: 64 (over z, y, core), rep: 4 (over x).
Axes of the slice: x: 4, y: 4, z: 8, core: 2. Of those that a mesh axis runs over, the one named last changes fastest.
Arguments:
- gradients: bfloat16 [4, 8, 512, 20480], P('rep', None, 'fsdp'), may hold values from -6 to 6
- second_moment: float32 [8, 512, 20480], P(None, 'fsdp', 'rep')
- left_roots: float32 [64, 3, 4, 512, 512], P('fsdp', None, 'rep')
- right_roots: float32 [64, 3, 4, 512, 512], P('fsdp', None, 'rep')
- owners: int32 [320], replicated, may hold values from 0 to 63, as said below
Outputs:
- update: bfloat16 [8, 512, 20480], P(None, 'fsdp')
Inputs may be any that keep to these rules, and one draw needn't show every extreme that they name: `owners`: an owner's blocks take its slots 0, 1, 2 ... in increasing block order; every owner holds 1 to 12 blocks, and some owner exactly 12.
All inputs are finite; a program needn't handle non-finite values.
Results may differ from a plain program's by a relative error of at most 0.015.
Values may be sent and summed in bfloat16 or wider, within the bound.
A program may use at most 128 MiB of HBM per device.

v0:
```python
import jax
import jax.numpy as jnp
from jax import lax
from jax.sharding import PartitionSpec as P

moment_decay = 0.999
adam_eps = 1e-08
norm_eps = 1e-06
learn_rate = 0.05


def slot_table(owners, slot_total, fsdp_count):
    block_count = owners.shape[0]
    positions = jnp.arange(block_count, dtype=jnp.int32)
    same_owner = (owners[:, None] == owners[None, :]) & (positions[None, :] < positions[:, None])
    slot_of = jnp.sum(same_owner.astype(jnp.int32), axis=1)
    holder_pos = owners * slot_total + slot_of
    places = jnp.arange(fsdp_count * slot_total, dtype=jnp.int32)
    matches = holder_pos[None, :] == places[:, None]
    holder = jnp.sum(jnp.where(matches, positions[None, :] + 1, 0), axis=1) - 1
    return (holder_pos, holder)


def pick_blocks(strips, chosen, col_blocks):
    filled = chosen >= 0
    safe_ids = jnp.where(filled, chosen, 0)
    picked = strips[safe_ids // col_blocks, :, safe_ids % col_blocks, :]
    return jnp.where(filled[..., None, None], picked, jnp.zeros((), strips.dtype))


def shards(gradients, second_moment, left_roots, right_roots, owners):
    fsdp_count = lax.axis_size("fsdp")
    rep_count = lax.axis_size("rep")
    rep_index = lax.axis_index("rep")
    owner_index = lax.axis_index("fsdp")
    grad_rows = gradients[0]
    row_blocks, rows_dev, width_all = grad_rows.shape
    block_size = left_roots.shape[-1]
    slot_rep = left_roots.shape[1]
    slot_total = slot_rep * rep_count
    col_blocks = width_all // block_size
    block_total = row_blocks * col_blocks
    quarter_width = second_moment.shape[2]
    holder_pos, holder = slot_table(owners, slot_total, fsdp_count)
    holder_grid = holder.reshape(fsdp_count, slot_rep, rep_count)
    summed = lax.psum(grad_rows.astype(jnp.float32).astype(jnp.bfloat16), "rep").astype(jnp.float32)
    own_cols = lax.dynamic_slice_in_dim(summed, rep_index * quarter_width, quarter_width, 2)
    own_ids = lax.dynamic_index_in_dim(holder_grid, rep_index, 2, keepdims=False).T
    strips = summed.reshape(row_blocks, rows_dev, col_blocks, block_size)
    outgoing = pick_blocks(strips, own_ids, col_blocks).reshape(
        slot_rep, fsdp_count * rows_dev, block_size
    )
    moment = moment_decay * second_moment + (1.0 - moment_decay) * own_cols * own_cols
    adam_dir = own_cols / (jnp.sqrt(moment) + adam_eps)
    column_sums = jnp.sum(adam_dir * adam_dir, axis=1)
    columns = rep_index * quarter_width + jnp.arange(quarter_width, dtype=jnp.int32)
    membership = (
        columns[:, None] // block_size == jnp.arange(col_blocks, dtype=jnp.int32)[None, :]
    ).astype(jnp.float32)
    partial_value = jnp.dot(
        column_sums, membership, precision=lax.Precision.HIGHEST, preferred_element_type=jnp.float32
    )
    adam_norm = jnp.sqrt(lax.psum(partial_value.reshape(block_total), ("fsdp", "rep")))
    arriving = lax.all_to_all(
        outgoing.astype(jnp.bfloat16), "fsdp", split_axis=1, concat_axis=1, tiled=True
    ).astype(outgoing.dtype)
    left_local = left_roots[0, :, 0]
    right_local = right_roots[0, :, 0]
    half_way = jnp.einsum(
        "kab,kbc->kac",
        left_local,
        arriving,
        precision=lax.Precision.HIGHEST,
        preferred_element_type=jnp.float32,
    )
    precond = jnp.einsum(
        "kab,kbc->kac",
        half_way,
        right_local,
        precision=lax.Precision.HIGHEST,
        preferred_element_type=jnp.float32,
    )
    owner_row = lax.dynamic_index_in_dim(holder_grid, owner_index, 0, keepdims=False)
    my_ids = lax.dynamic_index_in_dim(owner_row, rep_index, 1, keepdims=False)
    target = jnp.sum(
        jnp.where(
            my_ids[:, None] == jnp.arange(block_total, dtype=jnp.int32)[None, :],
            adam_norm[None, :],
            0.0,
        ),
        axis=1,
    )
    graft_ratio = target / (jnp.sqrt(jnp.sum(precond * precond, axis=(1, 2))) + norm_eps)
    scaled = (-learn_rate * precond * graft_ratio[:, None, None]).astype(jnp.bfloat16)
    widened = lax.all_gather(scaled, "rep", axis=0, tiled=True)
    collected = lax.all_to_all(widened, "fsdp", split_axis=1, concat_axis=1, tiled=True)
    pieces = collected.reshape(rep_count, slot_rep, fsdp_count, rows_dev, block_size)
    pieces = pieces.transpose(2, 1, 0, 3, 4).reshape(fsdp_count * slot_total, rows_dev, block_size)
    placed = jnp.take(pieces, holder_pos, axis=0)
    placed = placed.reshape(row_blocks, col_blocks, rows_dev, block_size).transpose(0, 2, 1, 3)
    return placed.reshape(row_blocks, rows_dev, width_all)


def solution(mesh):
    return jax.shard_map(
        shards,
        mesh=mesh,
        in_specs=(
            P("rep", None, "fsdp", None),
            P(None, "fsdp", "rep"),
            P("fsdp", None, "rep", None, None),
            P("fsdp", None, "rep", None, None),
            P(),
        ),
        out_specs=P(None, "fsdp", None),
        check_vma=False,
    )
```

profile of v0, /device:TPU:16, one launch (start us, length us, event | category | flops | bytes accessed | tf_op | source)
XLA Modules:
  0.0 513.8 jit_solution(17550033881851693876)
XLA Ops:
  6.5 0.0 copy-start
  6.5 0.0 copy-start.2
  6.5 0.0 all-reduce.2.cloned.1.call-start
  6.5 0.7 all-reduce.2.cloned.1.call-update
  7.3 0.1 copy-done.2
  7.4 0.2 convert_reduce_fusion
  7.6 0.2 select_reduce_fusion
  7.8 0.1 sub.19
  7.9 0.1 constant_dynamic-slice_fusion
  8.1 0.1 copy.27
  8.2 0.1 reshape.92
  8.3 0.1 broadcast_in_dim.80
  8.4 0.1 broadcast_in_dim.81
  8.5 76.4 %all-reduce.2.cloned.1.call-done = bf16[8,8,20480]{2,1,0:T(8,128)(2,1)} async-done(((bf16[8,8,20480]{2,1,0:T(8,128)(2,1)}), bf16[8,8,20480]{2,1,0:T(8,128)(2,1)}) %all-reduce.2.cloned.1.call-update) | async-done | bytes 2621456 | tf_op jit(solution)/shard_map/psum | solution.py:46
  84.9 4.4 convert_element_type.17
  89.3 5.5 %gather_fusion = bf16[192,8,512]{2,1,0:T(8,128)(2,1)} fusion(f32[8,8,40,512]{3,1,2,0:T(8,128)} %bitcast.36, s32[192]{0:T(256)S(1)} %reshape.92), kind=kCustom, calls=%fused_computation | custom fusion | bytes 3147264 | tf_op jit(solution)/shard_map/gather | solution.py:27
  94.8 1.8 fusion.4
  96.6 2.7 copy.28
  99.3 10.7 %all-to-all-start = ((bf16[3,512,512]{2,0,1:T(4,128)(2,1)}), bf16[3,512,512]{2,0,1:T(4,128)(2,1)}, u32[]{:S(2)}, u32[]{:S(2)}) async-start(bf16[3,512,512]{2,0,1:T(4,128)(2,1)} %copy.28), calls=%async_computation | async-start | bytes 4194304 | tf_op jit(solution)/shard_map/all_to_all | solution.py:64
  110.0 0.0 all-gather.2.cloned.1.call-start
  110.1 0.2 dynamic-slice_reduce_fusion
  110.3 2.7 fusion.11
  113.0 0.5 fusion.12
  113.4 0.1 reshape.88
  113.5 87.1 %psum.15 = f32[320]{0:T(512)S(1)} all-reduce(f32[320]{0:T(512)S(1)} %reshape.88), channel_id=1, replica_groups=mesh['fsdp'=64,'rep'=4] {'fsdp','rep'}, use_global_device_ids=true, to_apply=%region_4.5 | all-reduce | flops 320 | bytes 2560 | tf_op jit(solution)/shard_map/psum | solution.py:63
  200.7 0.2 select_reduce_fusion.1
  200.9 0.0 all-to-all-done
  200.9 5.4 %fusion.2 = f32[3,512,512]{1,2,0:T(8,128)S(1)} fusion(f32[1,3,1,512,512]{4,3,2,1,0:T(8,128)} %param.7, bf16[3,512,512]{2,0,1:T(4,128)(2,1)} %all-to-all-done), kind=kOutput, calls=%fused_computation.4 | convolution fusion | flops 4831838208 | bytes 7864320 | tf_op jit(solution)/shard_map/kab,kbc->kac/dot_general | solution.py:69
  206.2 0.0 copy-done
  206.2 5.7 %multiply_reduce_fusion = (f32[3]{0:T(128)S(1)}, f32[3,512,512]{2,1,0:T(8,128)S(1)}) fusion(f32[3,512,512]{1,2,0:T(8,128)S(1)} %fusion.2, f32[1,3,1,512,512]{4,3,2,1,0:T(8,128)S(1)} %copy-done), kind=kOutput, calls=%fused_computation.9 | convolution fusion | flops 4833411072 | bytes 9437196 | tf_op jit(solution)/shard_map/kab,kbc->kac/dot_general | solution.py:76
  212.0 1.7 multiply_convert_fusion
  213.6 0.0 all-gather.2.cloned.1.call-update
  213.7 66.8 %all-gather.2.cloned.1.call-done = bf16[12,512,512]{2,1,0:T(8,128)(2,1)} async-done(((bf16[3,512,512]{2,1,0:T(8,128)(2,1)}), bf16[12,512,512]{2,1,0:T(8,128)(2,1)}) %all-gather.2.cloned.1.call-update) | async-done | bytes 6291472 | tf_op jit(solution)/shard_map/all_gather | solution.py:95
  280.5 9.8 %copy.31 = bf16[12,512,512]{2,0,1:T(8,128)(2,1)} copy(bf16[12,512,512]{2,1,0:T(8,128)(2,1)} %all-gather.2.cloned.1.call-done) | data formatting | bytes 12582912 | tf_op jit(solution)/shard_map/all_gather | solution.py:95
  290.3 10.9 %all-to-all-start.1 = ((bf16[12,512,512]{2,0,1:T(8,128)(2,1)}), bf16[12,512,512]{2,0,1:T(8,128)(2,1)}, u32[]{:S(2)}, u32[]{:S(2)}) async-start(bf16[12,512,512]{2,0,1:T(8,128)(2,1)} %copy.31), calls=%async_computation.1 | async-start | bytes 16777216 | tf_op jit(solution)/shard_map/all_to_all | solution.py:96
  301.3 0.1 broadcast_in_dim.76
  301.4 186.3 %all-to-all-done.1 = bf16[12,512,512]{2,0,1:T(8,128)(2,1)} async-done(((bf16[12,512,512]{2,0,1:T(8,128)(2,1)}), bf16[12,512,512]{2,0,1:T(8,128)(2,1)}, u32[]{:S(2)}, u32[]{:S(2)}) %all-to-all-start.1) | async-done | bytes 6291488 | tf_op jit(solution)/shard_map/all_to_all | solution.py:96
  487.7 6.9 %copy.32 = bf16[12,512,512]{2,1,0:T(8,128)(2,1)S(1)} copy(bf16[12,512,512]{2,0,1:T(8,128)(2,1)} %all-to-all-done.1) | data formatting | bytes 12582912 | tf_op jit(solution)/shard_map/all_to_all | solution.py:96
  494.6 3.6 copy.33
  498.2 5.5 %gather_fusion.1 = bf16[320,8,512]{2,1,0:T(8,128)(2,1)} fusion(bf16[768,8,512]{2,1,0:T(8,128)(2,1)} %bitcast.35, s32[1024]{0:T(1024)S(1)} %pad_clamp_fusion), kind=kCustom, calls=%fused_computation.1 | custom fusion | bytes 5244160 | tf_op jit(solution)/shard_map/jit(_take)/gather | solution.py:99
  503.7 0.0 copy-start.1
  503.7 3.2 broadcast_select_fusion
  506.9 0.0 copy-done.1
  (10 shorter events, 0.1 us)
Async XLA Ops:
  6.5 199.7 %copy-start = (f32[1,3,1,512,512]{4,3,2,1,0:T(8,128)S(1)}, f32[1,3,1,512,512]{4,3,2,1,0:T(8,128)}, u32[]{:S(2)}) copy-start(f32[1,3,1,512,512]{4,3,2,1,0:T(8,128)} %param.8) | copy-start | bytes 9437188
  6.5 0.8 copy-start.2
  6.5 78.3 %all-reduce.2.cloned.1.call-start = ((), (), s32[]{:S(2)}) async-start(), calls=%async_computation.2 | async-start | bytes 5242880 | tf_op jit(solution)/shard_map/psum | solution.py:46
  99.3 101.6 %all-to-all-start = ((bf16[3,512,512]{2,0,1:T(4,128)(2,1)}), bf16[3,512,512]{2,0,1:T(4,128)(2,1)}, u32[]{:S(2)}, u32[]{:S(2)}) async-start(bf16[3,512,512]{2,0,1:T(4,128)(2,1)} %copy.28), calls=%async_computation | async-start | bytes 4194304 | tf_op jit(solution)/shard_map/all_to_all | solution.py:64
  110.0 170.5 %all-gather.2.cloned.1.call-start = ((), (), s32[]{:S(2)}) async-start(), calls=%async_computation.3 | async-start | bytes 7864320 | tf_op jit(solution)/shard_map/all_gather | solution.py:95
  290.3 197.4 %all-to-all-start.1 = ((bf16[12,512,512]{2,0,1:T(8,128)(2,1)}), bf16[12,512,512]{2,0,1:T(8,128)(2,1)}, u32[]{:S(2)}, u32[]{:S(2)}) async-start(bf16[12,512,512]{2,0,1:T(8,128)(2,1)} %copy.31), calls=%async_computation.1 | async-start | bytes 16777216 | tf_op jit(solution)/shard_map/all_to_all | solution.py:96
  503.7 3.2 copy-start.1
Sparse Core Ops, SparseCore 0:
  9.7 75.1 all-reduce.1
  213.8 66.6 all-gather.1
where the time goes:
time: 514 us
  waiting for transfers between devices  330 us (64%)
  blocking collectives  87.1 us (17%)
  local copies, waits for them, and re-layouts  35.2 us (7%)
  starting transfers between devices  21.7 us (4%)
  other arithmetic  14.4 us (3%)
  between operations  13.6 us (3%)
  matrix products  11.6 us (2%)
    all_to_all x1, waiting for transfers between devices, shards(): lax.all_to_all(widened, 'fsdp', split_axis=1, concat_axis=1, tiled=True)  186 us
    psum x1, blocking collectives, shards(): lax.psum(partial_value.reshape(block_total), ('fsdp', 'rep'))  87.1 us
    psum x1, waiting for transfers between devices, shards(): lax.psum(grad_rows.astype(jnp.float32).astype(jnp.bfloat16), 'rep')  76.4 us
    all_gather x1, waiting for transfers between devices, shards(): widened = lax.all_gather(scaled, 'rep', axis=0, tiled=True)  66.8 us
    all_to_all x1, starting transfers between devices, shards(): lax.all_to_all(widened, 'fsdp', split_axis=1, concat_axis=1, tiled=True)  10.9 us
    all_to_all x1, starting transfers between devices, shards(): lax.all_to_all(outgoing.astype(jnp.bfloat16), 'fsdp', split_axis=1, conca...  10.7 us
  transfers between devices with their start and end apart: 4, of which 3 were waited for; matrix products, arithmetic and copies ran while one was open for 1% of the time, Pallas kernels for 0%

commit v1 on v0

v1 whole, which is shorter than its diff:
```python
import functools
import jax
import jax.numpy as jnp
from jax import lax
from jax.experimental import pallas as pl
from jax.experimental.pallas import tpu as pltpu
from jax.sharding import PartitionSpec as P

moment_decay = 0.999
adam_eps = 1e-08
norm_eps = 1e-06
learn_rate = 0.05

BF = jnp.bfloat16
F32 = jnp.float32
MESH = pl.DeviceIdType.MESH
N_FSDP = 64
N_REP = 4
SLOTS = 3
NBLK = 320
COLB = 40
QCOL = 10
STRIP = (32, 128)
LIST = 240
CHUNKS = ((0, 32), (32, 32), (64, 32), (96, 32), (128, 32), (160, 40), (200, 40))
OUT_LIST = 160
OUT_AT = {1: 0, 0: 64, 2: 128}
OUT_LEN = {1: 64, 0: 64, 2: 32}
VMEM_LIMIT = 56 << 20


def owner_at(half, k):
    z = k // 4
    y = 2 * ((k // 2) % 2) + (z + half) % 2
    return z * 8 + y * 2 + k % 2


def split(x):
    hi = x.astype(BF)
    return hi, (x - hi.astype(F32)).astype(BF)


def mm(a, b):
    return jnp.dot(a, b, preferred_element_type=F32)


def exchange(ids, rank, slot2, grads, second, left, right, ag, sq,
             sa, ra, sb, rb, rb2, outgoing, arriving, g32, gbf, lbuf, rbuf, lhi, llo, rhi, rlo,
             pm, ps, u2, p2, acc, t1, t2, t3, n1, n2, n3,
             x_send, x_recv, a_send, a_recv, o_send, o_recv, g_send, g_recv, n_send, n_recv, loc):
    f = lax.axis_index("fsdp")
    r = lax.axis_index("rep")
    rt, lt, opp = (r + 1) % 4, (r + 3) % 4, (r + 2) % 4
    z, yc = f // 8, f % 8

    factor_copies = [pltpu.make_async_copy(left, lbuf, loc.at[0]), pltpu.make_async_copy(right, rbuf, loc.at[1])]
    for cp in factor_copies:
        cp.start()

    barrier = pltpu.get_barrier_semaphore()

    def greet(k, carry):
        pl.semaphore_signal(barrier, inc=1, device_id=((f + k) % N_FSDP, r), device_id_type=MESH)
        return carry

    lax.fori_loop(1, N_FSDP, greet, 0)
    for other in (rt, lt, opp):
        pl.semaphore_signal(barrier, inc=1, device_id=(f, other), device_id_type=MESH)

    def own(target, e):
        return grads[ids[target * LIST + e]]

    def own32(target, e):
        return own(target, e).astype(F32)

    def x_copy(c, kind, src, dst, to):
        return pltpu.make_async_remote_copy(src_ref=src, dst_ref=dst, send_sem=x_send.at[c, kind],
                                            recv_sem=x_recv.at[c, kind], device_id=(f, to), device_id_type=MESH)

    def rb_at(c, side, a, n):
        return rb2.at[side, pl.ds(a, n)] if c == 0 else rb.at[side, pl.ds(a, n)]

    def x_copies(c, kinds):
        lo, n = CHUNKS[c]
        h = n // 2
        every = (
            lambda: x_copy(c, 0, sa.at[pl.ds(lo, h)], ra.at[pl.ds(lo, h)], rt),
            lambda: x_copy(c, 1, sa.at[pl.ds(lo + h, h)], ra.at[pl.ds(lo + h, h)], lt),
            lambda: x_copy(c, 2, sb.at[0, pl.ds(lo + h, h)], rb_at(c, 0, lo + h, h), rt),
            lambda: x_copy(c, 3, sb.at[1, pl.ds(lo, h)], rb_at(c, 1, lo, h), lt),
            lambda: x_copy(c, 4, sb.at[0, pl.ds(lo, h)], rb_at(c, 0, lo, h), rt),
            lambda: x_copy(c, 5, sb.at[1, pl.ds(lo + h, h)], rb_at(c, 1, lo + h, h), lt),
        )
        return [every[k]() for k in kinds]

    def fill_a(c):
        lo, n = CHUNKS[c]
        h = n // 2

        def body(k, carry):
            sa[lo + k] = own(opp, lo + k)
            sa[lo + h + k] = own(opp, lo + h + k)
            sb[0, lo + h + k] = own(rt, lo + h + k)
            sb[1, lo + k] = own(lt, lo + k)
            return carry

        lax.fori_loop(0, h, body, 0, unroll=4)

    def step_a(c):
        fill_a(c)
        for cp in x_copies(c, (0, 1, 2, 3)):
            cp.start()

    def step_b(c):
        lo, n = CHUNKS[c]
        h = n // 2
        for cp in x_copies(c, (0, 1)):
            cp.wait_recv()

        def body(k, carry):
            e, g = lo + k, lo + h + k
            sb[0, e] = (own32(rt, e) + ra[e].astype(F32)).astype(BF)
            sb[1, g] = (own32(lt, g) + ra[g].astype(F32)).astype(BF)
            return carry

        lax.fori_loop(0, h, body, 0, unroll=4)
        for cp in x_copies(c, (4, 5)):
            cp.start()

    def wait_b(c):
        for cp in x_copies(c, (2, 3, 4, 5)):
            cp.wait_recv()

    def a_copy(s, d, k):
        return pltpu.make_async_remote_copy(src_ref=outgoing.at[s, d], dst_ref=arriving.at[s, f],
                                            send_sem=a_send.at[s, d], recv_sem=a_recv.at[s, f],
                                            device_id=(d, r), device_id_type=MESH)

    def a_go(s, d):
        @pl.when(d != f)
        def _():
            a_copy(s, d, 0).start()

        @pl.when(d == f)
        def _():
            arriving[s, f] = outgoing[s, d]

    def step_f(c):
        wait_b(c)
        if c == 0:
            def body(d, carry):
                p = rank[r * N_FSDP + d]
                total = own32(r, p) + rb2[0, p].astype(F32) + rb2[1, p].astype(F32)
                outgoing[2, d] = total.astype(BF)
                return carry

            lax.fori_loop(0, N_FSDP, body, 0, unroll=4)

            def go(k, carry):
                a_go(2, (f + k) % N_FSDP)
                return carry

            lax.fori_loop(0, N_FSDP, go, 0)
            return
        lo, n = CHUNKS[c]
        s, half = (c - 1) // 2, (c - 1) % 2

        def body(k, carry):
            e = lo + k
            total = own32(r, e) + rb[0, e].astype(F32) + rb[1, e].astype(F32)
            outgoing[s, owner_at(half, k)] = total.astype(BF)
            return carry

        lax.fori_loop(0, n, body, 0, unroll=4)

        def go(k, carry):
            a_go(s, owner_at(half, (z * 4 + k) % 32))
            return carry

        lax.fori_loop(0, n, go, 0)

    def prep(s):
        def body(k, carry):
            rows = pl.ds(pl.multiple_of(k * 64, 64), 64)
            lhi[s, rows, :], llo[s, rows, :] = split(lbuf[s, rows, :])
            rhi[s, rows, :], rlo[s, rows, :] = split(rbuf[s, rows, :])
            return carry

        lax.fori_loop(0, 8, body, 0)

    def product(s):
        def arrived(k, carry):
            src = (f + k) % N_FSDP
            pltpu.make_async_remote_copy(src_ref=outgoing.at[s, src], dst_ref=arriving.at[s, src],
                                         send_sem=a_send.at[s, src], recv_sem=a_recv.at[s, src],
                                         device_id=(src, r), device_id_type=MESH).wait_recv()
            return carry

        lax.fori_loop(1, N_FSDP, arrived, 0)

        def gather(m, carry):
            x = arriving[s, m].astype(F32)
            for t in range(4):
                g32[pl.ds(pl.multiple_of(m * 8, 8), 8), t * 128:(t + 1) * 128] = x[t * 8:(t + 1) * 8]
            return carry

        lax.fori_loop(0, N_FSDP, gather, 0, unroll=4)
        gbf[...] = g32[...].astype(BF)

        def rows_of(k, total):
            rows = pl.ds(pl.multiple_of(k * 128, 128), 128)
            half_way = mm(lhi[s, rows, :], gbf[...]) + mm(llo[s, rows, :], gbf[...])
            hhi, hlo = split(half_way)
            p = mm(hhi, rhi[s]) + (mm(hlo, rhi[s]) + mm(hhi, rlo[s]))
            pm[rows, :] = p
            q = p * p
            q = q.reshape(16, 8, 512).sum(axis=0)
            return total + (q[:, 0:128] + q[:, 128:256] + q[:, 256:384] + q[:, 384:512])

        total = lax.fori_loop(0, 4, rows_of, jnp.zeros((8, 128), F32))
        total = jnp.sum(jnp.sum(total, axis=0, keepdims=True), axis=1, keepdims=True)
        scale = -learn_rate / (jnp.sqrt(total) + norm_eps)

        def cut(m, carry):
            y = pm[pl.ds(pl.multiple_of(m * 8, 8), 8), :] * scale
            y = jnp.concatenate([y[:, t * 128:(t + 1) * 128] for t in range(4)], axis=0)
            ps[s, m] = y.astype(BF)
            return carry

        lax.fori_loop(0, N_FSDP, cut, 0, unroll=4)

    def o_copy(s, d, src):
        dst = u2.at[src] if s == 2 else ag.at[r, OUT_AT[s] + src]
        return pltpu.make_async_remote_copy(src_ref=ps.at[s, d], dst_ref=dst, send_sem=o_send.at[s, d],
                                            recv_sem=o_recv.at[s, src], device_id=(d, r), device_id_type=MESH)

    def o_self(s):
        dst = u2.at[f] if s == 2 else ag.at[r, OUT_AT[s] + f]
        return pltpu.make_async_copy(ps.at[s, f], dst, loc.at[2 + s])

    def send_out(s):
        o_self(s).start()

        def go(k, carry):
            o_copy(s, (f + k) % N_FSDP, f).start()
            return carry

        lax.fori_loop(1, N_FSDP, go, 0)

    def wait_out(s):
        o_self(s).wait()

        def arrived(k, carry):
            src = (f + k) % N_FSDP
            o_copy(s, src, src).wait_recv()
            return carry

        lax.fori_loop(1, N_FSDP, arrived, 0)

    def g_copy(s, kind, rep, a, n, to, src=None):
        here = ag.at[rep, pl.ds(OUT_AT[s] + a, n)]
        return pltpu.make_async_remote_copy(src_ref=here if src is None else src, dst_ref=here,
                                            send_sem=g_send.at[s, kind], recv_sem=g_recv.at[s, kind],
                                            device_id=(f, to), device_id_type=MESH)

    def g_copies(s, kinds):
        n = OUT_LEN[s]
        h = n // 2
        src = p2 if s == 2 else None
        every = (
            lambda: g_copy(s, 0, r, 0, n, rt, src),
            lambda: g_copy(s, 1, r, 0, n, lt, src),
            lambda: g_copy(s, 2, lt, 0, h, rt),
            lambda: g_copy(s, 3, rt, h, h, lt),
        )
        return [every[k]() for k in kinds]

    def own_two():
        return pltpu.make_async_copy(p2, ag.at[r, pl.ds(OUT_AT[2], OUT_LEN[2])], loc.at[5])

    def gather_one(s):
        wait_out(s)
        if s == 2:
            def body(p, carry):
                p2[p] = u2[slot2[r * 32 + p]]
                return carry

            lax.fori_loop(0, 32, body, 0, unroll=4)
            own_two().start()
        for cp in g_copies(s, (0, 1)):
            cp.start()

    def gather_two(s):
        for k in (0, 1):
            g_copies(s, (k,))[0].wait_recv()
            g_copies(s, (k + 2,))[0].start()

    def gather_end(s):
        for cp in g_copies(s, (2, 3)):
            cp.wait_recv()

    def adam():
        wait_b(5)
        wait_b(6)

        def body(k, carry):
            e = 160 + k
            total = own32(r, e) + rb[0, e].astype(F32) + rb[1, e].astype(F32)
            moment = moment_decay * second[k] + (1.0 - moment_decay) * total * total
            step = total / (jnp.sqrt(moment) + adam_eps)
            sums = jnp.sum(step * step, axis=0, keepdims=True)
            acc[pl.ds(k, 1), :] = sums
            return carry

        acc[pl.ds(80, 48), :] = jnp.zeros((48, 128), F32)
        lax.fori_loop(0, 80, body, 0, unroll=2)
        ones = jnp.ones((8, 128), F32)
        t1[...] = lax.dot_general(ones, acc[...], (((1,), (1,)), ((), ())),
                                  precision=lax.Precision.HIGHEST, preferred_element_type=F32)

    def n_copy(stage, k):
        if stage == 0:
            src, dst, to, at = t1, n1.at[yc], (z * 8 + (yc + k) % 8, r), k
        elif stage == 1:
            src, dst, to, at = t2, n2.at[z], (((z + k) % 8) * 8 + yc, r), 8 + k
        else:
            src, dst, to, at = t3, n3.at[r], (f, (r + k) % 4), 16 + k
        return pltpu.make_async_remote_copy(src_ref=src, dst_ref=dst, send_sem=n_send.at[at],
                                            recv_sem=n_recv.at[at], device_id=to, device_id_type=MESH)

    def n_start(stage):
        for k in range(1, 4 if stage == 2 else 8):
            n_copy(stage, k).start()

    def n_sum(stage):
        me, own_tile, got, out = ((yc, t1, n1, t2), (z, t2, n2, t3))[stage]
        got[me] = own_tile[...]
        for k in range(1, 8):
            n_copy(stage, k).wait_recv()
        out[...] = jnp.sum(got[...], axis=0)

    def n_end():
        n3[r] = t3[...]
        for k in range(1, 4):
            n_copy(2, k).wait_recv()
        sq[...] = n3[...]

    fill_a(0)
    pl.semaphore_wait(barrier, N_FSDP - 1 + 3)
    for cp in x_copies(0, (0, 1, 2, 3)):
        cp.start()
    step_a(1)
    step_b(0)
    step_a(2)
    step_f(0)
    step_b(1)
    step_a(3)
    step_f(1)
    step_b(2)
    step_a(4)
    for cp in factor_copies:
        cp.wait()
    step_f(2)
    step_b(3)
    prep(2)
    step_f(3)
    step_b(4)
    step_a(5)
    step_a(6)
    prep(0)
    prep(1)
    step_f(4)
    step_b(5)
    product(2)
    send_out(2)
    step_b(6)
    product(0)
    send_out(0)
    gather_one(2)
    product(1)
    send_out(1)
    adam()
    n_start(0)
    gather_two(2)
    n_sum(0)
    n_start(1)
    gather_one(0)
    gather_two(0)
    n_sum(1)
    n_start(2)
    gather_one(1)
    gather_two(1)
    n_end()
    own_two().wait()
    for s in (2, 0, 1):
        gather_end(s)

    for c in range(len(CHUNKS)):
        for cp in x_copies(c, range(6)):
            cp.wait_send()
    for s in range(SLOTS):
        def sent(k, carry, s=s):
            d = (f + k) % N_FSDP
            a_copy(s, d, k).wait_send()
            o_copy(s, d, f).wait_send()
            return carry

        lax.fori_loop(1, N_FSDP, sent, 0)
        for cp in g_copies(s, range(4)):
            cp.wait_send()
    for stage in range(3):
        for k in range(1, 4 if stage == 2 else 8):
            n_copy(stage, k).wait_send()


def place(pos, ag, sq, out, norm):
    ones = jnp.where(lax.broadcasted_iota(jnp.int32, (8, 128), 0) == 0, 1.0, 0.0).astype(F32)
    for q in range(N_REP):
        rows = lax.dot_general(sq[q], ones, (((0,), (0,)), ((), ())),
                               precision=lax.Precision.HIGHEST, preferred_element_type=F32)
        norm[q * 128:(q + 1) * 128, :] = jnp.sqrt(rows)

    def line(i, carry):
        for q in range(N_REP):
            for j in range(QCOL):
                b = i * COLB + q * QCOL + j
                scale = norm[pl.ds(q * 128 + i * QCOL + j, 1), :]
                out[b] = (ag[pos[b]].astype(F32) * scale).astype(BF)
        return carry

    lax.fori_loop(0, NBLK // COLB, line, 0)


def tables(owners):
    blocks = jnp.arange(NBLK, dtype=jnp.int32)
    earlier = (owners[:, None] == owners[None, :]) & (blocks[None, :] < blocks[:, None])
    slot = jnp.sum(earlier.astype(jnp.int32), axis=1)
    s, rep = slot // N_REP, slot % N_REP
    key = (s * N_REP + rep) * N_FSDP + owners
    places = jnp.arange(SLOTS * N_REP * N_FSDP, dtype=jnp.int32)
    holder = jnp.sum(jnp.where(key[None, :] == places[:, None], blocks[None, :] + 1, 0), axis=1) - 1
    holder = holder.reshape(SLOTS, N_REP, N_FSDP)
    filled = holder[2] >= 0
    people = jnp.arange(N_FSDP, dtype=jnp.int32)
    rank = jnp.sum((filled[:, None, :] & (people[None, None, :] < people[None, :, None])).astype(jnp.int32), axis=2)
    rank = jnp.minimum(rank, 31)
    at = (rank[:, :, None] == jnp.arange(32, dtype=jnp.int32)[None, None, :]) & filled[:, :, None]
    packed = jnp.sum(jnp.where(at, holder[2][:, :, None], 0), axis=1)
    slot2 = jnp.sum(jnp.where(at, people[None, :, None], 0), axis=1)
    order = [owner_at(half, k) for half in range(2) for k in range(32)]
    order = jnp.asarray(order, jnp.int32)
    safe = jnp.maximum(holder, 0)
    k = jnp.arange(80, dtype=jnp.int32)
    quarter = (k // QCOL) * COLB + k % QCOL
    quarter = quarter[None, :] + QCOL * jnp.arange(N_REP, dtype=jnp.int32)[:, None]
    ids = jnp.concatenate([packed, safe[0][:, order], safe[1][:, order], quarter], axis=1)
    rank_of = jnp.sum(jnp.where(rep[:, None] == jnp.arange(N_REP)[None, :], rank[:, owners].T, 0), axis=1)
    entry = jnp.where(s == 1, OUT_AT[1] + owners, jnp.where(s == 0, OUT_AT[0] + owners, OUT_AT[2] + rank_of))
    pos = rep * OUT_LIST + entry
    return ids.reshape(-1), rank.reshape(-1), slot2.reshape(-1), pos


def shards(gradients, second_moment, left_roots, right_roots, owners):
    ids, rank, slot2, pos = tables(owners)
    grads = gradients.reshape(8, 8, 160, 128).transpose(0, 2, 1, 3).reshape(NBLK, *STRIP)
    second = second_moment.reshape(8, 8, 40, 128).transpose(0, 2, 1, 3).reshape(80, *STRIP)
    left = left_roots.reshape(SLOTS, 512, 512)
    right = right_roots.reshape(SLOTS, 512, 512)
    smem = pl.BlockSpec(memory_space=pltpu.SMEM)
    vmem = pl.BlockSpec(memory_space=pltpu.VMEM)
    hbm = pl.BlockSpec(memory_space=pl.ANY)
    dma = pltpu.SemaphoreType.DMA
    vm = pltpu.VMEM
    chunks = len(CHUNKS)
    ag, sq = pl.pallas_call(
        exchange,
        out_shape=(
            jax.ShapeDtypeStruct((N_REP, OUT_LIST, *STRIP), BF),
            jax.ShapeDtypeStruct((N_REP, 8, 128), F32),
        ),
        in_specs=[smem, smem, smem, vmem, vmem, hbm, hbm],
        out_specs=(hbm, vmem),
        scratch_shapes=[
            vm((LIST, *STRIP), BF), vm((LIST, *STRIP), BF),
            vm((2, LIST, *STRIP), BF), vm((2, LIST, *STRIP), BF), vm((2, 32, *STRIP), BF),
            vm((SLOTS, N_FSDP, *STRIP), BF), vm((SLOTS, N_FSDP, *STRIP), BF),
            vm((512, 512), F32), vm((512, 512), BF),
            vm((SLOTS, 512, 512), F32), vm((SLOTS, 512, 512), F32),
            vm((SLOTS, 512, 512), BF), vm((SLOTS, 512, 512), BF),
            vm((SLOTS, 512, 512), BF), vm((SLOTS, 512, 512), BF),
            vm((512, 512), F32), vm((SLOTS, N_FSDP, *STRIP), BF),
            vm((N_FSDP, *STRIP), BF), vm((32, *STRIP), BF), vm((128, 128), F32),
            vm((8, 128), F32), vm((8, 128), F32), vm((8, 128), F32),
            vm((8, 8, 128), F32), vm((8, 8, 128), F32), vm((N_REP, 8, 128), F32),
            dma((chunks, 6)), dma((chunks, 6)),
            dma((SLOTS, N_FSDP)), dma((SLOTS, N_FSDP)),
            dma((SLOTS, N_FSDP)), dma((SLOTS, N_FSDP)),
            dma((SLOTS, 4)), dma((SLOTS, 4)),
            dma((20,)), dma((20,)), dma((6,)),
        ],
        compiler_params=pltpu.CompilerParams(collective_id=0, has_side_effects=True, vmem_limit_bytes=VMEM_LIMIT),
        name="exchange",
    )(ids, rank, slot2, grads, second, left, right)
    out = pl.pallas_call(
        place,
        out_shape=jax.ShapeDtypeStruct((NBLK, *STRIP), BF),
        in_specs=[smem, vmem, vmem],
        out_specs=vmem,
        scratch_shapes=[vm((N_REP * 128, 128), F32)],
        compiler_params=pltpu.CompilerParams(vmem_limit_bytes=VMEM_LIMIT),
        name="place",
    )(pos, ag.reshape(N_REP * OUT_LIST, *STRIP), sq)
    return out.reshape(8, 160, 8, 128).transpose(0, 2, 1, 3).reshape(8, 8, 20480)


def solution(mesh):
    return jax.shard_map(
        shards,
        mesh=mesh,
        in_specs=(
            P("rep", None, "fsdp", None),
            P(None, "fsdp", "rep"),
            P("fsdp", None, "rep", None, None),
            P("fsdp", None, "rep", None, None),
            P(),
        ),
        out_specs=P(None, "fsdp", None),
        check_vma=False,
    )
```

time: 514 us -> 165 us (0.32)
  waiting for transfers between devices: 330 us -> 0 us
  Pallas kernels: 0 us -> 153 us
  blocking collectives: 87.1 us -> 0 us
  local copies, waits for them, and re-layouts: 35.2 us -> 5 us
  starting transfers between devices: 21.7 us -> 0 us
  between operations: 13.6 us -> 0.09 us
  matrix products: 11.6 us -> 0 us
  other arithmetic: 14.4 us -> 4.57 us
    all_to_all x2 -> x0, waiting for transfers between devices: 186 us -> none  [the longest x1 186 us: shards(): lax.all_to_all(widened, 'fsdp', split_axis=1, concat_axis=1, tiled=True)]
    pallas_call x0 -> x2, Pallas kernels: none -> 153 us  [the longest x1 148 us: shards(): pl.pallas_call(exchange, out_shape=(jax.ShapeDtypeStruct((N_REP, OUT_LIST...]
    psum x1 -> x0, blocking collectives: 87.1 us -> none  [shards(): lax.psum(partial_value.reshape(block_total), ('fsdp', 'rep'))]
    psum x1 -> x0, waiting for transfers between devices: 76.4 us -> none  [shards(): lax.psum(grad_rows.astype(jnp.float32).astype(jnp.bfloat16), 'rep')]
    all_gather x1 -> x0, waiting for transfers between devices: 66.8 us -> none  [shards(): widened = lax.all_gather(scaled, 'rep', axis=0, tiled=True)]
    all_to_all x2 -> x0, starting transfers between devices: 21.7 us -> none  [the longest x1 10.9 us: shards(): lax.all_to_all(widened, 'fsdp', split_axis=1, concat_axis=1, tiled=True)]
    dot_general x3 -> x0, matrix products: 11.6 us -> none  [the longest x1 5.72 us: shards(): jnp.einsum('kab,kbc->kac', half_way, right_local, precision=lax.Precision...]
    all_gather x1 -> x0, local copies, waits for them, and re-layouts: 9.82 us -> none  [shards(): widened = lax.all_gather(scaled, 'rep', axis=0, tiled=True)]
  transfers between devices with their start and end apart: 4 -> 0, of which waited for: 3 -> 0; matrix products, arithmetic and copies ran while one was open for 1% -> 0% of each run, Pallas kernels for 0% -> 0%
where the time goes in v1:
time: 165 us; the launch traced here: 163 us
  Pallas kernels  153 us (93%)
  local copies, waits for them, and re-layouts  5 us (3%)
  other arithmetic  4.57 us (3%)
    pallas_call x1, Pallas kernels, shards(): pl.pallas_call(exchange, out_shape=(jax.ShapeDtypeStruct((N_REP, OUT_LIST...  148 us
    pallas_call x1, Pallas kernels, shards(): pl.pallas_call(place, out_shape=jax.ShapeDtypeStruct((NBLK, *STRIP), BF),...  4.92 us

profile of v1, /device:TPU:16, one launch (start us, length us, event | category | flops | bytes accessed | tf_op | source)
XLA Modules:
  0.0 163.0 jit_solution(7610339753322992375)
XLA Ops:
  0.0 0.1 broadcast_add_fusion.1
  0.1 1.0 convert_reduce_fusion
  1.1 0.7 pad_clamp_fusion
  1.7 0.7 add_select_fusion.1
  2.4 0.2 select_reduce_fusion
  2.7 0.1 ge.11
  2.8 0.2 convert_reduce_fusion.1
  2.9 0.7 min.16.rank
  3.6 0.1 broadcast_in_dim.69
  3.7 0.1 squeeze.7
  3.8 0.2 select_reduce_fusion.2
  4.0 0.6 reshape.138.slot2
  4.6 0.1 squeeze.8
  4.7 0.1 copy.25
  4.8 0.6 gather_fusion.2
  5.4 0.1 copy.27
  5.4 0.1 copy.23
  5.5 0.1 copy.24
  5.6 0.6 gather_fusion.1
  6.2 0.1 copy.26
  6.3 0.1 pad_add_fusion
  6.4 0.7 reshape.137.ids
  7.1 1.1 gather_fusion
  8.1 0.2 select_reduce_fusion.1
  8.4 1.3 fusion.3.pos
  9.6 148.5 %exchange.1 = (bf16[4,160,32,128]{3,2,1,0:T(8,128)(2,1)}, f32[4,8,128]{2,1,0:T(8,128)}) custom-call(s32[960]{0:T(1024)} %reshape.137.ids, s32[256]{0:T(256)} %min.16.rank, s32[128]{0:T(128)} %reshape.138.slot2, bf16[320,32,128]{2,1,0:T(8,128)(2,1)} %bitcast.23, f32[80,32,128]{2,1,0:T(8,128)} %bitcast.24, f32[3,512,512]{2,1,0:T(8,128)} %bitcast.21, ...), custom_call_target="tpu_custom_call" | custom-call | tf_op jit(solution)/shard_map/exchange/pallas_call | solution.py:475
  158.1 4.9 %place.1 = bf16[320,32,128]{2,1,0:T(8,128)(2,1)} custom-call(s32[320]{0:T(512)} %fusion.3.pos, bf16[640,32,128]{2,1,0:T(8,128)(2,1)} %bitcast.20, f32[4,8,128]{2,1,0:T(8,128)} %get-tuple-element.8.sq), custom_call_target="tpu_custom_call" | custom-call | tf_op jit(solution)/shard_map/place/pallas_call | solution.py:504
  (9 shorter events, 0.1 us)

commit v2 on v0

v2 whole, which is shorter than its diff:
```python
import functools
import jax
import jax.numpy as jnp
from jax import lax
from jax.experimental import pallas as pl
from jax.experimental.pallas import tpu as pltpu
from jax.sharding import PartitionSpec as P

moment_decay = 0.999
adam_eps = 1e-08
norm_eps = 1e-06
learn_rate = 0.05

BF = jnp.bfloat16
F32 = jnp.float32
MESH = pl.DeviceIdType.MESH
N_FSDP = 64
N_REP = 4
NBLK = 320
SLOTS = 3
COLB = 40
QCOL = 10
HALF = (16, 128)
PACKED = 64
LIST = 208
CHUNKS = ((0, 64, 0, 0), (64, 64, 0, 1), (128, 64, 64, 0), (192, 64, 64, 1), (256, 80, 128, 0), (336, 80, 128, 1))
ENTRIES = 416
PARTS = 4
RANK, WHO, POS = 4, 6, 7
VMEM_LIMIT = 56 << 20


def split(x):
    hi = x.astype(BF)
    return hi, (x - hi.astype(F32)).astype(BF)


def mm(a, b):
    return jnp.dot(a, b, preferred_element_type=F32)


def exchange(tab, grads, second, left, right, ag, sq,
             sa, ra, sb, rb, rbp0, rbp1, outgoing, arriving, g32, gbf, lbuf, rbuf, lhi, llo, rhi, rlo, vbuf,
             pm, ps, u0, u1, pk, acc, t1, t2, t3, n1, n2, n3,
             x_send, x_recv, a_send, a_recv, o_send, o_recv, g_send, g_recv, n_send, n_recv, loc):
    f = lax.axis_index("fsdp")
    r = lax.axis_index("rep")
    rt, lt, opp = (r + 1) % 4, (r + 3) % 4, (r + 2) % 4
    z, yc = f // 8, f % 8
    peer = ((f + 1) % N_FSDP, r)
    rbp, u = (rbp0, rbp1), (u0, u1)

    barrier = pltpu.get_barrier_semaphore()
    for other in (rt, lt, opp):
        pl.semaphore_signal(barrier, inc=1, device_id=(f, other), device_id_type=MESH)

    def greet(k, carry):
        pl.semaphore_signal(barrier, inc=1, device_id=((f + k) % N_FSDP, r), device_id_type=MESH)
        return carry

    lax.fori_loop(1, N_FSDP, greet, 0)

    loads = [pltpu.make_async_copy(left, lbuf, loc.at[0]), pltpu.make_async_copy(right, rbuf, loc.at[1]),
             pltpu.make_async_copy(second, vbuf, loc.at[2])]
    for cp in loads:
        cp.start()

    def own(c, target, k):
        return grads[tab[target, CHUNKS[c][2] + k], CHUNKS[c][3]]

    def own32(c, target, k):
        return own(c, target, k).astype(F32)

    def remote(src, dst, send, recv, to):
        return pltpu.make_async_remote_copy(src_ref=src, dst_ref=dst, send_sem=send, recv_sem=recv,
                                            device_id=to, device_id_type=MESH)

    def rb_at(c, side, k, n):
        return rbp[c].at[side, pl.ds(k, n)] if c < 2 else rb.at[side, pl.ds(CHUNKS[c][0] + k, n)]

    def x_copies(c, kinds):
        lo, n = CHUNKS[c][:2]
        h = n // 2
        first, last = pl.ds(lo, h), pl.ds(lo + h, h)
        right_to, left_to = (f, rt), (f, lt)
        one, two = x_recv.at[c, 0], x_recv.at[c, 1]
        every = (
            lambda: remote(sa.at[first], ra.at[first], x_send.at[0], one, right_to),
            lambda: remote(sa.at[last], ra.at[last], x_send.at[0], one, left_to),
            lambda: remote(sb.at[0, last], rb_at(c, 0, h, h), x_send.at[1], two, right_to),
            lambda: remote(sb.at[1, first], rb_at(c, 1, 0, h), x_send.at[2], two, left_to),
            lambda: remote(sb.at[0, first], rb_at(c, 0, 0, h), x_send.at[1], two, right_to),
            lambda: remote(sb.at[1, last], rb_at(c, 1, h, h), x_send.at[2], two, left_to),
        )
        return [every[k]() for k in kinds]

    def fill_a(c):
        lo, n = CHUNKS[c][:2]
        h = n // 2

        def body(k, carry):
            sa[lo + k] = own(c, opp, k)
            sa[lo + h + k] = own(c, opp, h + k)
            sb[0, lo + h + k] = own(c, rt, h + k)
            sb[1, lo + k] = own(c, lt, k)
            return carry

        lax.fori_loop(0, h, body, 0, unroll=4)

    def send_a(c):
        for cp in x_copies(c, (0, 1, 2, 3)):
            cp.start()

    def step_a(c):
        fill_a(c)
        send_a(c)

    def step_b(c):
        lo, n = CHUNKS[c][:2]
        h = n // 2
        both = pl.ds(lo, n)
        remote(sa.at[both], ra.at[both], x_send.at[0], x_recv.at[c, 0], (f, rt)).wait_recv()

        def body(k, carry):
            e, g = lo + k, lo + h + k
            sb[0, e] = (own32(c, rt, k) + ra[e].astype(F32)).astype(BF)
            sb[1, g] = (own32(c, lt, h + k) + ra[g].astype(F32)).astype(BF)
            return carry

        lax.fori_loop(0, h, body, 0, unroll=4)
        for cp in x_copies(c, (4, 5)):
            cp.start()

    def wait_b(c):
        lo, n = CHUNKS[c][:2]
        both = sb.at[:, pl.ds(lo, n)]
        remote(both, both, x_send.at[1], x_recv.at[c, 1], (f, rt)).wait_recv()

    def most(s, half, buf, send, recv):
        part = buf.at[s, half, pl.ds(0, N_FSDP - 1)]
        return remote(part, part, send.at[s, half], recv.at[s, half], peer)

    def to_owners(s, half, total):
        def body(k, carry):
            d = (f + k) % N_FSDP
            outgoing[s, half, d] = total(d).astype(BF)
            remote(outgoing.at[s, half, d], arriving.at[s, half, f], a_send.at[s, half], a_recv.at[s, half],
                   (d, r)).start()
            return carry

        lax.fori_loop(1, N_FSDP, body, 0, unroll=3)
        arriving[s, half, f] = total(f).astype(BF)

    def step_f(half):
        c = 2 + half
        lo = CHUNKS[c][0]
        wait_b(c)
        to_owners(0, half, lambda d: own32(c, r, d) + rb[0, lo + d].astype(F32) + rb[1, lo + d].astype(F32))

    def step_p(half):
        got = rbp[half]
        wait_b(half)
        for s in (1, 2):
            def total(d, s=s):
                p = tab[RANK + s - 1, r * N_FSDP + d]
                return own32(half, r, p) + got[0, p].astype(F32) + got[1, p].astype(F32)

            to_owners(s, half, total)

    def prep(s):
        def body(k, carry):
            rows = pl.ds(pl.multiple_of(k * 64, 64), 64)
            lhi[s, rows, :], llo[s, rows, :] = split(lbuf[s, rows, :])
            rhi[s, rows, :], rlo[s, rows, :] = split(rbuf[s, rows, :])
            return carry

        lax.fori_loop(0, 8, body, 0)

    def product(s):
        for half in range(2):
            most(s, half, arriving, a_send, a_recv).wait_recv()

            def gather(m, carry, half=half):
                x = arriving[s, half, m].astype(F32)
                for t in range(2):
                    cols = slice(half * 256 + t * 128, half * 256 + (t + 1) * 128)
                    g32[pl.ds(pl.multiple_of(m * 8, 8), 8), cols] = x[t * 8:(t + 1) * 8]
                return carry

            lax.fori_loop(0, N_FSDP, gather, 0, unroll=4)
        gbf[...] = g32[...].astype(BF)

        def rows_of(k, total):
            rows = pl.ds(pl.multiple_of(k * 128, 128), 128)
            half_way = mm(lhi[s, rows, :], gbf[...]) + mm(llo[s, rows, :], gbf[...])
            hhi, hlo = split(half_way)
            p = mm(hhi, rhi[s]) + (mm(hlo, rhi[s]) + mm(hhi, rlo[s]))
            pm[s, rows, :] = p
            q = p * p
            q = q.reshape(16, 8, 512).sum(axis=0)
            return total + (q[:, 0:128] + q[:, 128:256] + q[:, 256:384] + q[:, 384:512])

        total = lax.fori_loop(0, 4, rows_of, jnp.zeros((8, 128), F32))
        total = jnp.sum(jnp.sum(total, axis=0, keepdims=True), axis=1, keepdims=True)
        return -learn_rate / (jnp.sqrt(total) + norm_eps)

    def landing(s, half, src):
        return ag.at[r, half, src] if s == 0 else u[half].at[s - 1, src]

    def o_self(s, half):
        return pltpu.make_async_copy(ps.at[s, half, f], landing(s, half, f), loc.at[3 + s * 2 + half])

    def send_out(s, half, scale):
        def cut(d):
            y = pm[s, pl.ds(pl.multiple_of(d * 8, 8), 8), half * 256:(half + 1) * 256] * scale
            ps[s, half, d] = jnp.concatenate([y[:, 0:128], y[:, 128:256]], axis=0).astype(BF)

        def go(k, carry):
            d = (f + k) % N_FSDP
            cut(d)
            remote(ps.at[s, half, d], landing(s, half, f), o_send.at[s, half], o_recv.at[s, half], (d, r)).start()
            return carry

        lax.fori_loop(1, N_FSDP, go, 0, unroll=3)
        cut(f)
        o_self(s, half).start()

    def wait_out(s, half):
        o_self(s, half).wait()
        most(s, half, ps, o_send, o_recv).wait_recv()

    def g_copy(part, kind, rep, a, n, to):
        here = ag.at[rep, part, pl.ds(a, n)]
        src = pk.at[part - 2] if part >= 2 and kind < 2 else here
        return remote(src, here, g_send.at[part], g_recv.at[part, min(kind, 2)], (f, to))

    def g_copies(part, kinds):
        every = (
            lambda: g_copy(part, 0, r, 0, 64, rt),
            lambda: g_copy(part, 1, r, 0, 64, lt),
            lambda: g_copy(part, 2, lt, 0, 32, rt),
            lambda: g_copy(part, 3, rt, 32, 32, lt),
        )
        return [every[k]() for k in kinds]

    def own_packed(half):
        return pltpu.make_async_copy(pk.at[half], ag.at[r, 2 + half], loc.at[9 + half])

    def gather_one(part):
        half = part % 2
        if part < 2:
            wait_out(0, half)
        else:
            wait_out(1, half)
            wait_out(2, half)

            def body(p, carry):
                pk[half, p] = u[half].reshape(128, *HALF)[tab[WHO, r * PACKED + p]]
                return carry

            lax.fori_loop(0, PACKED, body, 0, unroll=4)
            own_packed(half).start()
        for cp in g_copies(part, (0, 1)):
            cp.start()

    def gather_two(part):
        for k in (0, 1):
            g_copies(part, (k,))[0].wait_recv()
            g_copies(part, (k + 2,))[0].start()

    def gather_end(part):
        g_copy(part, 2, opp, 0, 64, rt).wait_recv()

    def adam():
        wait_b(4)
        wait_b(5)

        def one(c, k):
            lo = CHUNKS[c][0]
            return own32(c, r, k) + rb[0, lo + k].astype(F32) + rb[1, lo + k].astype(F32)

        def body(k, carry):
            total = jnp.concatenate([one(4, k), one(5, k)], axis=0)
            moment = moment_decay * vbuf[k] + (1.0 - moment_decay) * total * total
            step = total / (jnp.sqrt(moment) + adam_eps)
            acc[pl.ds(k, 1), :] = jnp.sum(step * step, axis=0, keepdims=True)
            return carry

        acc[pl.ds(80, 48), :] = jnp.zeros((48, 128), F32)
        lax.fori_loop(0, 80, body, 0, unroll=2)
        ones = jnp.ones((8, 128), F32)
        t1[...] = lax.dot_general(ones, acc[...], (((1,), (1,)), ((), ())),
                                  precision=lax.Precision.HIGHEST, preferred_element_type=F32)

    def n_parts(stage):
        return ((yc, t1, n1, t2), (z, t2, n2, t3), (r, t3, n3, None))[stage]

    def n_start(stage):
        me, tile, got, _ = n_parts(stage)
        for k in range(1, 4 if stage == 2 else 8):
            to = ((z * 8 + (yc + k) % 8, r), (((z + k) % 8) * 8 + yc, r), (f, (r + k) % 4))[stage]
            remote(tile, got.at[me], n_send.at[stage], n_recv.at[stage], to).start()
        got[me] = tile[...]

    def n_all(stage):
        got = n_parts(stage)[2]
        part = got.at[pl.ds(0, 3 if stage == 2 else 7)]
        return remote(part, part, n_send.at[stage], n_recv.at[stage], peer)

    def n_sum(stage):
        n_all(stage).wait_recv()
        _, _, got, out = n_parts(stage)
        if stage == 2:
            sq[...] = got[...]
        else:
            out[...] = jnp.sum(got[...], axis=0)

    fill_a(0)
    fill_a(1)
    pl.semaphore_wait(barrier, N_FSDP - 1 + 3)
    send_a(0)
    send_a(1)
    step_b(0)
    step_a(2)
    step_b(1)
    step_p(0)
    step_a(3)
    step_b(2)
    step_p(1)
    for cp in loads:
        cp.wait()
    prep(1)
    step_b(3)
    step_f(0)
    step_a(4)
    prep(2)
    scale1 = product(1)
    send_out(1, 0, scale1)
    step_f(1)
    scale2 = product(2)
    send_out(2, 0, scale2)
    send_out(1, 1, scale1)
    send_out(2, 1, scale2)
    step_b(4)
    step_a(5)
    prep(0)
    scale0 = product(0)
    send_out(0, 0, scale0)
    send_out(0, 1, scale0)
    step_b(5)
    gather_one(2)
    gather_one(3)
    gather_two(2)
    adam()
    n_start(0)
    gather_two(3)
    gather_one(0)
    n_sum(0)
    n_start(1)
    gather_two(0)
    gather_one(1)
    n_sum(1)
    n_start(2)
    gather_two(1)
    n_sum(2)
    for half in range(2):
        own_packed(half).wait()
    for part in (2, 3, 0, 1):
        gather_end(part)

    remote(sa, sa, x_send.at[0], x_recv.at[0, 0], (f, rt)).wait_send()
    for side in range(2):
        remote(sb.at[side], sb.at[side], x_send.at[1 + side], x_recv.at[0, 0], (f, rt)).wait_send()
    for s in range(SLOTS):
        for half in range(2):
            most(s, half, outgoing, a_send, a_recv).wait_send()
            most(s, half, ps, o_send, o_recv).wait_send()
    for part in range(PARTS):
        three = ag.at[pl.ds(0, 3), part]
        remote(three, three, g_send.at[part], g_recv.at[part, 0], (f, rt)).wait_send()
    for stage in range(3):
        n_all(stage).wait_send()


def place(tab, ag, sq, out, norm):
    ones = jnp.where(lax.broadcasted_iota(jnp.int32, (8, 128), 0) == 0, 1.0, 0.0).astype(F32)
    for q in range(N_REP):
        rows = lax.dot_general(sq[q], ones, (((0,), (0,)), ((), ())),
                               precision=lax.Precision.HIGHEST, preferred_element_type=F32)
        norm[q * 128:(q + 1) * 128, :] = jnp.sqrt(rows)

    def line(i, carry):
        for q in range(N_REP):
            for j in range(QCOL):
                b = i * COLB + q * QCOL + j
                scale = norm[pl.ds(q * 128 + i * QCOL + j, 1), :]
                p = tab[POS, b]
                for half in range(2):
                    out[b, half] = (ag[p + half * 64].astype(F32) * scale).astype(BF)
        return carry

    lax.fori_loop(0, NBLK // COLB, line, 0)


def tables(owners, tab):
    row = owners[...]
    sub = lax.broadcasted_iota(jnp.int32, (NBLK, NBLK), 0)
    lane = lax.broadcasted_iota(jnp.int32, (NBLK, NBLK), 1)

    def down(mask, value=1):
        return jnp.sum(jnp.where(mask, value, 0), axis=0, keepdims=True)

    def along(mask, value=1):
        return jnp.sum(jnp.where(mask, value, 0), axis=1, keepdims=True)

    col = along(sub == lane, row)
    same = col == row
    slot_c = along(same & (lane < sub))
    slot_r = down(same & (sub < lane))
    key_c, key_r = slot_c * N_FSDP + col, slot_r * N_FSDP + row
    alike = (slot_c & 3) == (slot_r & 3)
    rank_c = along(alike & (slot_r >= 4) & (key_r < key_c))
    rank_r = down(alike & (slot_c >= 4) & (key_c < key_r))
    code = jnp.where(slot_c < 4, key_c, 1024 + (slot_c & 3) * PACKED + rank_c)
    e = lax.broadcasted_iota(jnp.int32, (1, 256), 1)
    block = lax.broadcasted_iota(jnp.int32, (NBLK, 1), 0)
    a = e - 128
    line = sum(jnp.where(a >= QCOL * i, 1, 0) for i in range(1, 8))
    for t in range(N_REP):
        want = jnp.where(e < 64, 1024 + t * PACKED + e, t * N_FSDP + e - 64)
        found = down(code == want, block)
        mine = line * COLB + t * QCOL + a - line * QCOL
        tab[t:t + 1, 0:256] = jnp.where(e < 128, found, jnp.where(e < LIST, mine, 0))
    for s in (1, 2):
        tab[RANK + s - 1:RANK + s, 0:256] = down(key_c == s * 256 + e, rank_c)
    tab[WHO:WHO + 1, 0:256] = down(code == 1024 + e, ((slot_c >> 2) - 1) * N_FSDP + col)
    tab[POS:POS + 1, 0:NBLK] = (slot_r & 3) * 256 + jnp.where(slot_r < 4, row, 128 + rank_r)


def shards(gradients, second_moment, left_roots, right_roots, owners):
    grads = gradients.reshape(8, 8, 160, 128).transpose(0, 2, 1, 3).reshape(NBLK, 2, *HALF)
    second = second_moment.reshape(8, 8, 40, 128).transpose(0, 2, 1, 3).reshape(80, 32, 128)
    left = left_roots.reshape(SLOTS, 512, 512)
    right = right_roots.reshape(SLOTS, 512, 512)
    smem = pl.BlockSpec(memory_space=pltpu.SMEM)
    vmem = pl.BlockSpec(memory_space=pltpu.VMEM)
    hbm = pl.BlockSpec(memory_space=pl.ANY)
    dma = pltpu.SemaphoreType.DMA
    vm = pltpu.VMEM
    tab = pl.pallas_call(
        tables,
        out_shape=jax.ShapeDtypeStruct((8, 384), jnp.int32),
        in_specs=[vmem],
        out_specs=vmem,
        name="tables",
    )(owners.reshape(1, NBLK))
    ag, sq = pl.pallas_call(
        exchange,
        out_shape=(
            jax.ShapeDtypeStruct((N_REP, PARTS, 64, *HALF), BF),
            jax.ShapeDtypeStruct((N_REP, 8, 128), F32),
        ),
        in_specs=[smem, vmem, hbm, hbm, hbm],
        out_specs=(hbm, vmem),
        scratch_shapes=[
            vm((ENTRIES, *HALF), BF), vm((ENTRIES, *HALF), BF),
            vm((2, ENTRIES, *HALF), BF), vm((2, ENTRIES, *HALF), BF),
            vm((2, PACKED, *HALF), BF), vm((2, PACKED, *HALF), BF),
            vm((SLOTS, 2, N_FSDP, *HALF), BF), vm((SLOTS, 2, N_FSDP, *HALF), BF),
            vm((512, 512), F32), vm((512, 512), BF),
            vm((SLOTS, 512, 512), F32), vm((SLOTS, 512, 512), F32),
            vm((SLOTS, 512, 512), BF), vm((SLOTS, 512, 512), BF),
            vm((SLOTS, 512, 512), BF), vm((SLOTS, 512, 512), BF), vm((80, 32, 128), F32),
            vm((SLOTS, 512, 512), F32), vm((SLOTS, 2, N_FSDP, *HALF), BF),
            vm((2, N_FSDP, *HALF), BF), vm((2, N_FSDP, *HALF), BF), vm((2, PACKED, *HALF), BF), vm((128, 128), F32),
            vm((8, 128), F32), vm((8, 128), F32), vm((8, 128), F32),
            vm((8, 8, 128), F32), vm((8, 8, 128), F32), vm((N_REP, 8, 128), F32),
            dma((3,)), dma((len(CHUNKS), 2)),
            dma((SLOTS, 2)), dma((SLOTS, 2)), dma((SLOTS, 2)), dma((SLOTS, 2)),
            dma((PARTS,)), dma((PARTS, 3)), dma((3,)), dma((3,)), dma((11,)),
        ],
        compiler_params=pltpu.CompilerParams(collective_id=0, has_side_effects=True, vmem_limit_bytes=VMEM_LIMIT),
        name="exchange",
    )(tab, grads, second, left, right)
    out = pl.pallas_call(
        place,
        out_shape=jax.ShapeDtypeStruct((NBLK, 2, *HALF), BF),
        in_specs=[smem, vmem, vmem],
        out_specs=vmem,
        scratch_shapes=[vm((N_REP * 128, 128), F32)],
        compiler_params=pltpu.CompilerParams(vmem_limit_bytes=VMEM_LIMIT),
        name="place",
    )(tab, ag.reshape(N_REP * PARTS * 64, *HALF), sq)
    return out.reshape(8, 160, 8, 128).transpose(0, 2, 1, 3).reshape(8, 8, 20480)


def solution(mesh):
    return jax.shard_map(
        shards,
        mesh=mesh,
        in_specs=(
            P("rep", None, "fsdp", None),
            P(None, "fsdp", "rep"),
            P("fsdp", None, "rep", None, None),
            P("fsdp", None, "rep", None, None),
            P(),
        ),
        out_specs=P(None, "fsdp", None),
        check_vma=False,
    )
```

time: 514 us -> 134 us (0.26)
  waiting for transfers between devices: 330 us -> 0 us
  Pallas kernels: 0 us -> 131 us
  blocking collectives: 87.1 us -> 0 us
  local copies, waits for them, and re-layouts: 35.2 us -> 1.24 us
  starting transfers between devices: 21.7 us -> 0 us
  other arithmetic: 14.4 us -> 0 us
  between operations: 13.6 us -> 0.01 us
  matrix products: 11.6 us -> 0 us
    all_to_all x2 -> x0, waiting for transfers between devices: 186 us -> none  [the longest x1 186 us: shards(): lax.all_to_all(widened, 'fsdp', split_axis=1, concat_axis=1, tiled=True)]
    pallas_call x0 -> x3, Pallas kernels: none -> 131 us  [the longest x1 124 us: shards(): pl.pallas_call(exchange, out_shape=(jax.ShapeDtypeStruct((N_REP, PARTS, 6...]
    psum x1 -> x0, blocking collectives: 87.1 us -> none  [shards(): lax.psum(partial_value.reshape(block_total), ('fsdp', 'rep'))]
    psum x1 -> x0, waiting for transfers between devices: 76.4 us -> none  [shards(): lax.psum(grad_rows.astype(jnp.float32).astype(jnp.bfloat16), 'rep')]
    all_gather x1 -> x0, waiting for transfers between devices: 66.8 us -> none  [shards(): widened = lax.all_gather(scaled, 'rep', axis=0, tiled=True)]
    all_to_all x2 -> x0, starting transfers between devices: 21.7 us -> none  [the longest x1 10.9 us: shards(): lax.all_to_all(widened, 'fsdp', split_axis=1, concat_axis=1, tiled=True)]
    dot_general x3 -> x0, matrix products: 11.6 us -> none  [the longest x1 5.72 us: shards(): jnp.einsum('kab,kbc->kac', half_way, right_local, precision=lax.Precision...]
    gather x2 -> x0, local copies, waits for them, and re-layouts: 11 us -> none  [the longest x1 5.52 us: pick_blocks(): picked = strips[safe_ids // col_blocks, :, safe_ids % col_blocks, :]]
  transfers between devices with their start and end apart: 4 -> 0, of which waited for: 3 -> 0; matrix products, arithmetic and copies ran while one was open for 1% -> 0% of each run, Pallas kernels for 0% -> 0%
where the time goes in v2:
time: 134 us; the launch traced here: 133 us
  Pallas kernels  131 us (98%)
    pallas_call x1, Pallas kernels, shards(): pl.pallas_call(exchange, out_shape=(jax.ShapeDtypeStruct((N_REP, PARTS, 6...  124 us
    pallas_call x1, Pallas kernels, shards(): pl.pallas_call(place, out_shape=jax.ShapeDtypeStruct((NBLK, 2, *HALF), BF...  4.97 us

profile of v2, /device:TPU:16, one launch (start us, length us, event | category | flops | bytes accessed | tf_op | source)
XLA Modules:
  0.0 132.6 jit_solution(7742044889606370299)
XLA Ops:
  0.0 1.2 reshape.30.owners
  1.2 2.0 %tables.1.tab = s32[8,384]{1,0:T(8,128)} custom-call(s32[1,320]{1,0:T(1,128)} %reshape.30.owners), custom_call_target="tpu_custom_call" | custom-call | tf_op jit(solution)/shard_map/tables/pallas_call | solution.py:450
  3.3 124.4 %exchange.1 = (bf16[4,4,64,16,128]{4,3,2,1,0:T(8,128)(2,1)}, f32[4,8,128]{2,1,0:T(8,128)}) custom-call(s32[8,384]{1,0:T(8,128)} %tables.1.tab, bf16[320,2,16,128]{3,2,1,0:T(8,128)(2,1)} %bitcast.21, f32[80,32,128]{2,1,0:T(8,128)} %bitcast.22, f32[3,512,512]{2,1,0:T(8,128)} %bitcast.19, f32[3,512,512]{2,1,0:T(8,128)} %bitcast.20), custom_call_target="tpu_custom_call" | custom-call | tf_op jit(solution)/shard_map/exchange/pallas_call | solution.py:457
  127.7 5.0 %place.1 = bf16[320,2,16,128]{3,2,1,0:T(8,128)(2,1)} custom-call(s32[8,384]{1,0:T(8,128)} %tables.1.tab, bf16[1024,16,128]{2,1,0:T(8,128)(2,1)} %bitcast.18, f32[4,8,128]{2,1,0:T(8,128)} %get-tuple-element.8.sq), custom_call_target="tpu_custom_call" | custom-call | tf_op jit(solution)/shard_map/place/pallas_call | solution.py:485

commit v3 on v2

--- a/solution.py
+++ b/solution.py
@@ -42,7 +42,7 @@
 def exchange(tab, grads, second, left, right, ag, sq,
              sa, ra, sb, rb, rbp0, rbp1, outgoing, arriving, g32, gbf, lbuf, rbuf, lhi, llo, rhi, rlo, vbuf,
              pm, ps, u0, u1, pk, acc, t1, t2, t3, n1, n2, n3,
-             x_send, x_recv, a_send, a_recv, o_send, o_recv, g_send, g_recv, n_send, n_recv, loc):
+             x_send, x_recv, a_send, a_recv, o_send, o_recv, g_send, g_recv, n_send, n_recv, loc, lines):
     f = lax.axis_index("fsdp")
     r = lax.axis_index("rep")
     rt, lt, opp = (r + 1) % 4, (r + 3) % 4, (r + 2) % 4
@@ -53,12 +53,9 @@
     barrier = pltpu.get_barrier_semaphore()
     for other in (rt, lt, opp):
         pl.semaphore_signal(barrier, inc=1, device_id=(f, other), device_id_type=MESH)
-
-    def greet(k, carry):
-        pl.semaphore_signal(barrier, inc=1, device_id=((f + k) % N_FSDP, r), device_id_type=MESH)
-        return carry
-
-    lax.fori_loop(1, N_FSDP, greet, 0)
+    for k in range(1, 8):
+        pl.semaphore_signal(barrier, inc=1, device_id=(z * 8 + (yc + k) % 8, r), device_id_type=MESH)
+        pl.semaphore_signal(barrier, inc=1, device_id=(((z + k) % 8) * 8 + yc, r), device_id_type=MESH)
 
     loads = [pltpu.make_async_copy(left, lbuf, loc.at[0]), pltpu.make_async_copy(right, rbuf, loc.at[1]),
              pltpu.make_async_copy(second, vbuf, loc.at[2])]
@@ -111,10 +108,6 @@
         for cp in x_copies(c, (0, 1, 2, 3)):
             cp.start()
 
-    def step_a(c):
-        fill_a(c)
-        send_a(c)
-
     def step_b(c):
         lo, n = CHUNKS[c][:2]
         h = n // 2
@@ -225,6 +218,9 @@
         cut(f)
         o_self(s, half).start()
 
+    def out_sent(s, half):
+        most(s, half, ps, o_send, o_recv).wait_send()
+
     def wait_out(s, half):
         o_self(s, half).wait()
         most(s, half, ps, o_send, o_recv).wait_recv()
@@ -317,50 +313,61 @@
 
     fill_a(0)
     fill_a(1)
-    pl.semaphore_wait(barrier, N_FSDP - 1 + 3)
-    send_a(0)
-    send_a(1)
-    step_b(0)
-    step_a(2)
-    step_b(1)
-    step_p(0)
-    step_a(3)
-    step_b(2)
-    step_p(1)
     for cp in loads:
         cp.wait()
     prep(1)
+    pl.semaphore_wait(barrier, 3 + 7 + 7)
+    for k in range(1, 8):
+        pl.semaphore_signal(lines, inc=1, device_id=(z * 8 + (yc + k) % 8, r), device_id_type=MESH)
+    send_a(0)
+    fill_a(2)
+    prep(2)
+    step_b(0)
+    send_a(1)
+    fill_a(3)
+    pl.semaphore_wait(lines, 7)
+    step_p(0)
+    step_b(1)
+    send_a(2)
+    step_p(1)
+    step_b(2)
+    send_a(3)
     step_b(3)
+    fill_a(4)
+    send_a(4)
     step_f(0)
-    step_a(4)
-    prep(2)
+    step_f(1)
+    step_b(4)
+    fill_a(5)
+    prep(0)
     scale1 = product(1)
     send_out(1, 0, scale1)
-    step_f(1)
     scale2 = product(2)
     send_out(2, 0, scale2)
+    send_a(5)
+    scale0 = product(0)
+    out_sent(1, 0)
+    send_out(0, 0, scale0)
+    step_b(5)
+    out_sent(2, 0)
     send_out(1, 1, scale1)
+    gather_one(2)
+    out_sent(0, 0)
     send_out(2, 1, scale2)
-    step_b(4)
-    step_a(5)
-    prep(0)
-    scale0 = product(0)
-    send_out(0, 0, scale0)
+    gather_two(2)
+    gather_one(0)
+    out_sent(1, 1)
     send_out(0, 1, scale0)
-    step_b(5)
-    gather_one(2)
-    gather_one(3)
-    gather_two(2)
     adam()
     n_start(0)
-    gather_two(3)
-    gather_one(0)
+    gather_two(0)
+    gather_one(3)
     n_sum(0)
     n_start(1)
-    gather_two(0)
-    gather_one(1)
+    gather_two(3)
     n_sum(1)
     n_start(2)
+    gather_one(1)
     gather_two(1)
     n_sum(2)
     for half in range(2):
@@ -374,7 +381,8 @@
     for s in range(SLOTS):
         for half in range(2):
             most(s, half, outgoing, a_send, a_recv).wait_send()
-            most(s, half, ps, o_send, o_recv).wait_send()
+    out_sent(2, 1)
+    out_sent(0, 1)
     for part in range(PARTS):
         three = ag.at[pl.ds(0, 3), part]
         remote(three, three, g_send.at[part], g_recv.at[part, 0], (f, rt)).wait_send()
@@ -403,7 +411,7 @@
 
 
 def tables(owners, tab):
-    row = owners[...]
+    row = owners[...].reshape(1, NBLK)
     sub = lax.broadcasted_iota(jnp.int32, (NBLK, NBLK), 0)
     lane = lax.broadcasted_iota(jnp.int32, (NBLK, NBLK), 1)
 
@@ -453,7 +461,7 @@
         in_specs=[vmem],
         out_specs=vmem,
         name="tables",
-    )(owners.reshape(1, NBLK))
+    )(owners)
     ag, sq = pl.pallas_call(
         exchange,
         out_shape=(
@@ -477,7 +485,7 @@
             vm((8, 8, 128), F32), vm((8, 8, 128), F32), vm((N_REP, 8, 128), F32),
             dma((3,)), dma((len(CHUNKS), 2)),
             dma((SLOTS, 2)), dma((SLOTS, 2)), dma((SLOTS, 2)), dma((SLOTS, 2)),
-            dma((PARTS,)), dma((PARTS, 3)), dma((3,)), dma((3,)), dma((11,)),
+            dma((PARTS,)), dma((PARTS, 3)), dma((3,)), dma((3,)), dma((11,)), pltpu.SemaphoreType.REGULAR,
         ],
         compiler_params=pltpu.CompilerParams(collective_id=0, has_side_effects=True, vmem_limit_bytes=VMEM_LIMIT),
         name="exchange",

time: 134 us -> 125 us (0.933)
  Pallas kernels: 131 us -> 123 us
    pallas_call x1, Pallas kernels: 124 us -> 116 us  [shards(): pl.pallas_call(exchange, out_shape=(jax.ShapeDtypeStruct((N_REP, PARTS, 6...]
where the time goes in v3:
time: 125 us; the launch traced here: 123 us
  Pallas kernels  123 us (98%)
    pallas_call x1, Pallas kernels, shards(): pl.pallas_call(exchange, out_shape=(jax.ShapeDtypeStruct((N_REP, PARTS, 6...  116 us
    pallas_call x1, Pallas kernels, shards(): pl.pallas_call(place, out_shape=jax.ShapeDtypeStruct((NBLK, 2, *HALF), BF...  4.97 us

profile of v3, /device:TPU:16, one launch (start us, length us, event | category | flops | bytes accessed | tf_op | source)
XLA Modules:
  0.0 123.1 jit_solution(8423513038256955445)
XLA Ops:
  0.0 2.0 %tables.1.tab = s32[8,384]{1,0:T(8,128)} custom-call(s32[320]{0:T(512)} %owners.1), custom_call_target="tpu_custom_call" | custom-call | tf_op jit(solution)/shard_map/tables/pallas_call | solution.py:458
  2.0 116.1 %exchange.1 = (bf16[4,4,64,16,128]{4,3,2,1,0:T(8,128)(2,1)}, f32[4,8,128]{2,1,0:T(8,128)}) custom-call(s32[8,384]{1,0:T(8,128)} %tables.1.tab, bf16[320,2,16,128]{3,2,1,0:T(8,128)(2,1)} %bitcast.21, f32[80,32,128]{2,1,0:T(8,128)} %bitcast.22, f32[3,512,512]{2,1,0:T(8,128)} %bitcast.19, f32[3,512,512]{2,1,0:T(8,128)} %bitcast.20), custom_call_target="tpu_custom_call" | custom-call | tf_op jit(solution)/shard_map/exchange/pallas_call | solution.py:465
  118.1 5.0 %place.1 = bf16[320,2,16,128]{3,2,1,0:T(8,128)(2,1)} custom-call(s32[8,384]{1,0:T(8,128)} %tables.1.tab, bf16[1024,16,128]{2,1,0:T(8,128)(2,1)} %bitcast.18, f32[4,8,128]{2,1,0:T(8,128)} %get-tuple-element.8.sq), custom_call_target="tpu_custom_call" | custom-call | tf_op jit(solution)/shard_map/place/pallas_call | solution.py:493

commit v4 on v3

--- a/solution.py
+++ b/solution.py
@@ -39,8 +39,8 @@
     return jnp.dot(a, b, preferred_element_type=F32)
 
 
-def exchange(tab, grads, second, left, right, ag, sq,
-             sa, ra, sb, rb, rbp0, rbp1, outgoing, arriving, g32, gbf, lbuf, rbuf, lhi, llo, rhi, rlo, vbuf,
+def exchange(tab, grads_in, second, left, right, ag, sq,
+             grads, sa, ra, sb, rb, rbp0, rbp1, outgoing, arriving, g32, gbf, lbuf, rbuf, lhi, llo, rhi, rlo, vbuf,
              pm, ps, u0, u1, pk, acc, t1, t2, t3, n1, n2, n3,
              x_send, x_recv, a_send, a_recv, o_send, o_recv, g_send, g_recv, n_send, n_recv, loc, lines):
     f = lax.axis_index("fsdp")
@@ -49,6 +49,9 @@
     z, yc = f // 8, f % 8
     peer = ((f + 1) % N_FSDP, r)
     rbp, u = (rbp0, rbp1), (u0, u1)
+
+    grads_copy = pltpu.make_async_copy(grads_in, grads, loc.at[11])
+    grads_copy.start()
 
     barrier = pltpu.get_barrier_semaphore()
     for other in (rt, lt, opp):
@@ -311,64 +314,65 @@
         else:
             out[...] = jnp.sum(got[...], axis=0)
 
+    grads_copy.wait()
     fill_a(0)
+    pl.semaphore_wait(barrier, 3 + 7 + 7)
+    send_a(0)
+    for k in range(1, 8):
+        pl.semaphore_signal(lines, inc=1, device_id=(z * 8 + (yc + k) % 8, r), device_id_type=MESH)
     fill_a(1)
     for cp in loads:
         cp.wait()
     prep(1)
-    pl.semaphore_wait(barrier, 3 + 7 + 7)
-    for k in range(1, 8):
-        pl.semaphore_signal(lines, inc=1, device_id=(z * 8 + (yc + k) % 8, r), device_id_type=MESH)
-    send_a(0)
+    step_b(0)
+    send_a(1)
     fill_a(2)
     prep(2)
-    step_b(0)
-    send_a(1)
-    fill_a(3)
     pl.semaphore_wait(lines, 7)
     step_p(0)
     step_b(1)
+    fill_a(3)
     send_a(2)
     step_p(1)
     step_b(2)
     send_a(3)
+    fill_a(4)
+    prep(0)
     step_b(3)
-    fill_a(4)
     send_a(4)
     step_f(0)
+    fill_a(5)
     step_f(1)
-    step_b(4)
-    fill_a(5)
-    prep(0)
     scale1 = product(1)
     send_out(1, 0, scale1)
     scale2 = product(2)
     send_out(2, 0, scale2)
+    step_b(4)
     send_a(5)
     scale0 = product(0)
     out_sent(1, 0)
     send_out(0, 0, scale0)
     step_b(5)
     out_sent(2, 0)
-    send_out(1, 1, scale1)
+    send_out(0, 1, scale0)
     gather_one(2)
     out_sent(0, 0)
-    send_out(2, 1, scale2)
+    send_out(1, 1, scale1)
     gather_two(2)
     gather_one(0)
-    out_sent(1, 1)
-    send_out(0, 1, scale0)
+    out_sent(0, 1)
+    send_out(2, 1, scale2)
     adam()
     n_start(0)
     gather_two(0)
-    gather_one(3)
+    gather_one(1)
     n_sum(0)
     n_start(1)
-    gather_two(3)
+    gather_two(1)
     n_sum(1)
     n_start(2)
-    gather_one(1)
-    gather_two(1)
+    gather_one(3)
+    gather_two(3)
     n_sum(2)
     for half in range(2):
         own_packed(half).wait()
@@ -381,8 +385,8 @@
     for s in range(SLOTS):
         for half in range(2):
             most(s, half, outgoing, a_send, a_recv).wait_send()
+    out_sent(1, 1)
     out_sent(2, 1)
-    out_sent(0, 1)
     for part in range(PARTS):
         three = ag.at[pl.ds(0, 3), part]
         remote(three, three, g_send.at[part], g_recv.at[part, 0], (f, rt)).wait_send()
@@ -390,24 +394,36 @@
         n_all(stage).wait_send()
 
 
-def place(tab, ag, sq, out, norm):
+def place(tab, ag, sq, out, norm, buf, res, came, left):
+    loads = [[pltpu.make_async_copy(ag.at[:, kind * 2 + half], buf.at[half, :, kind], came.at[half, kind])
+              for kind in range(2)] for half in range(2)]
+    for pair in loads:
+        for cp in pair:
+            cp.start()
     ones = jnp.where(lax.broadcasted_iota(jnp.int32, (8, 128), 0) == 0, 1.0, 0.0).astype(F32)
     for q in range(N_REP):
         rows = lax.dot_general(sq[q], ones, (((0,), (0,)), ((), ())),
                                precision=lax.Precision.HIGHEST, preferred_element_type=F32)
         norm[q * 128:(q + 1) * 128, :] = jnp.sqrt(rows)
 
-    def line(i, carry):
-        for q in range(N_REP):
-            for j in range(QCOL):
-                b = i * COLB + q * QCOL + j
-                scale = norm[pl.ds(q * 128 + i * QCOL + j, 1), :]
-                p = tab[POS, b]
-                for half in range(2):
-                    out[b, half] = (ag[p + half * 64].astype(F32) * scale).astype(BF)
-        return carry
-
-    lax.fori_loop(0, NBLK // COLB, line, 0)
+    for half in range(2):
+        for cp in loads[half]:
+            cp.wait()
+        entries = buf.at[half].reshape(N_REP * 128, *HALF)
+
+        def line(i, carry, half=half, entries=entries):
+            for q in range(N_REP):
+                for j in range(QCOL):
+                    b = i * COLB + q * QCOL + j
+                    scale = norm[pl.ds(q * 128 + i * QCOL + j, 1), :]
+                    res[half, b] = (entries[tab[POS, b]].astype(F32) * scale).astype(BF)
+            mine = pl.ds(i * COLB, COLB)
+            pltpu.make_async_copy(res.at[half, mine], out.at[mine, half], left.at[half]).start()
+            return carry
+
+        lax.fori_loop(0, NBLK // COLB, line, 0)
+    for half in range(2):
+        pltpu.make_async_copy(res.at[half], out.at[:, half], left.at[half]).wait()
 
 
 def tables(owners, tab):
@@ -442,7 +458,7 @@
     for s in (1, 2):
         tab[RANK + s - 1:RANK + s, 0:256] = down(key_c == s * 256 + e, rank_c)
     tab[WHO:WHO + 1, 0:256] = down(code == 1024 + e, ((slot_c >> 2) - 1) * N_FSDP + col)
-    tab[POS:POS + 1, 0:NBLK] = (slot_r & 3) * 256 + jnp.where(slot_r < 4, row, 128 + rank_r)
+    tab[POS:POS + 1, 0:NBLK] = (slot_r & 3) * 128 + jnp.where(slot_r < 4, row, 64 + rank_r)
 
 
 def shards(gradients, second_moment, left_roots, right_roots, owners):
@@ -468,10 +484,10 @@
             jax.ShapeDtypeStruct((N_REP, PARTS, 64, *HALF), BF),
             jax.ShapeDtypeStruct((N_REP, 8, 128), F32),
         ),
-        in_specs=[smem, vmem, hbm, hbm, hbm],
+        in_specs=[smem, hbm, hbm, hbm, hbm],
         out_specs=(hbm, vmem),
         scratch_shapes=[
-            vm((ENTRIES, *HALF), BF), vm((ENTRIES, *HALF), BF),
+            vm((NBLK, 2, *HALF), BF), vm((ENTRIES, *HALF), BF), vm((ENTRIES, *HALF), BF),
             vm((2, ENTRIES, *HALF), BF), vm((2, ENTRIES, *HALF), BF),
             vm((2, PACKED, *HALF), BF), vm((2, PACKED, *HALF), BF),
             vm((SLOTS, 2, N_FSDP, *HALF), BF), vm((SLOTS, 2, N_FSDP, *HALF), BF),
@@ -485,7 +501,7 @@
             vm((8, 8, 128), F32), vm((8, 8, 128), F32), vm((N_REP, 8, 128), F32),
             dma((3,)), dma((len(CHUNKS), 2)),
             dma((SLOTS, 2)), dma((SLOTS, 2)), dma((SLOTS, 2)), dma((SLOTS, 2)),
-            dma((PARTS,)), dma((PARTS, 3)), dma((3,)), dma((3,)), dma((11,)), pltpu.SemaphoreType.REGULAR,
+            dma((PARTS,)), dma((PARTS, 3)), dma((3,)), dma((3,)), dma((12,)), pltpu.SemaphoreType.REGULAR,
         ],
         compiler_params=pltpu.CompilerParams(collective_id=0, has_side_effects=True, vmem_limit_bytes=VMEM_LIMIT),
         name="exchange",
@@ -493,12 +509,13 @@
     out = pl.pallas_call(
         place,
         out_shape=jax.ShapeDtypeStruct((NBLK, 2, *HALF), BF),
-        in_specs=[smem, vmem, vmem],
-        out_specs=vmem,
-        scratch_shapes=[vm((N_REP * 128, 128), F32)],
+        in_specs=[smem, hbm, vmem],
+        out_specs=hbm,
+        scratch_shapes=[vm((N_REP * 128, 128), F32), vm((2, N_REP, 2, 64, *HALF), BF), vm((2, NBLK, *HALF), BF),
+                        dma((2, 2)), dma((2,))],
         compiler_params=pltpu.CompilerParams(vmem_limit_bytes=VMEM_LIMIT),
         name="place",
-    )(tab, ag.reshape(N_REP * PARTS * 64, *HALF), sq)
+    )(tab, ag, sq)
     return out.reshape(8, 160, 8, 128).transpose(0, 2, 1, 3).reshape(8, 8, 20480)
 
 

time: 125 us -> 122 us (0.976)
  Pallas kernels: 123 us -> 120 us
    pallas_call x1, Pallas kernels: 116 us -> 113 us  [shards(): pl.pallas_call(exchange, out_shape=(jax.ShapeDtypeStruct((N_REP, PARTS, 6...]
where the time goes in v4:
time: 122 us; the launch traced here: 120 us
  Pallas kernels  120 us (98%)
    pallas_call x1, Pallas kernels, shards(): pl.pallas_call(exchange, out_shape=(jax.ShapeDtypeStruct((N_REP, PARTS, 6...  113 us
    pallas_call x1, Pallas kernels, shards(): pl.pallas_call(place, out_shape=jax.ShapeDtypeStruct((NBLK, 2, *HALF), BF...  4.78 us

profile of v4, /device:TPU:16, one launch (start us, length us, event | category | flops | bytes accessed | tf_op | source)
XLA Modules:
  0.0 119.9 jit_solution(2698934177369590049)
XLA Ops:
  0.0 2.0 %tables.1.tab = s32[8,384]{1,0:T(8,128)} custom-call(s32[320]{0:T(512)} %owners.1), custom_call_target="tpu_custom_call" | custom-call | tf_op jit(solution)/shard_map/tables/pallas_call | solution.py:474
  2.0 113.1 %exchange.1 = (bf16[4,4,64,16,128]{4,3,2,1,0:T(8,128)(2,1)}, f32[4,8,128]{2,1,0:T(8,128)}) custom-call(s32[8,384]{1,0:T(8,128)} %tables.1.tab, bf16[320,2,16,128]{3,2,1,0:T(8,128)(2,1)} %bitcast.19, f32[80,32,128]{2,1,0:T(8,128)} %bitcast.20, f32[3,512,512]{2,1,0:T(8,128)} %bitcast.17, f32[3,512,512]{2,1,0:T(8,128)} %bitcast.18), custom_call_target="tpu_custom_call" | custom-call | tf_op jit(solution)/shard_map/exchange/pallas_call | solution.py:481
  115.1 4.8 %place.1 = bf16[320,2,16,128]{3,2,1,0:T(8,128)(2,1)} custom-call(s32[8,384]{1,0:T(8,128)} %tables.1.tab, bf16[4,4,64,16,128]{4,3,2,1,0:T(8,128)(2,1)} %get-tuple-element.7.ag, f32[4,8,128]{2,1,0:T(8,128)} %get-tuple-element.8.sq), custom_call_target="tpu_custom_call" | custom-call | tf_op jit(solution)/shard_map/place/pallas_call | solution.py:509

commit v5 on v4

--- a/solution.py
+++ b/solution.py
@@ -358,19 +358,19 @@
     gather_one(2)
     out_sent(0, 0)
     send_out(1, 1, scale1)
+    adam()
+    n_start(0)
     gather_two(2)
     gather_one(0)
     out_sent(0, 1)
     send_out(2, 1, scale2)
-    adam()
-    n_start(0)
-    gather_two(0)
-    gather_one(1)
     n_sum(0)
     n_start(1)
-    gather_two(1)
+    gather_two(0)
     n_sum(1)
     n_start(2)
+    gather_one(1)
+    gather_two(1)
     gather_one(3)
     gather_two(3)
     n_sum(2)

time: 122 us -> 122 us (level)
  no operation moved by 1% of the time
where the time goes in v5:
time: 122 us; the launch traced here: 120 us
  Pallas kernels  120 us (98%)
    pallas_call x1, Pallas kernels, shards(): pl.pallas_call(exchange, out_shape=(jax.ShapeDtypeStruct((N_REP, PARTS, 6...  113 us
    pallas_call x1, Pallas kernels, shards(): pl.pallas_call(place, out_shape=jax.ShapeDtypeStruct((NBLK, 2, *HALF), BF...  4.78 us

profile of v5, /device:TPU:16, one launch (start us, length us, event | category | flops | bytes accessed | tf_op | source)
XLA Modules:
  0.0 119.6 jit_solution(16578816648159890975)
XLA Ops:
  0.0 2.0 %tables.1.tab = s32[8,384]{1,0:T(8,128)} custom-call(s32[320]{0:T(512)} %owners.1), custom_call_target="tpu_custom_call" | custom-call | tf_op jit(solution)/shard_map/tables/pallas_call | solution.py:474
  2.0 112.8 %exchange.1 = (bf16[4,4,64,16,128]{4,3,2,1,0:T(8,128)(2,1)}, f32[4,8,128]{2,1,0:T(8,128)}) custom-call(s32[8,384]{1,0:T(8,128)} %tables.1.tab, bf16[320,2,16,128]{3,2,1,0:T(8,128)(2,1)} %bitcast.19, f32[80,32,128]{2,1,0:T(8,128)} %bitcast.20, f32[3,512,512]{2,1,0:T(8,128)} %bitcast.17, f32[3,512,512]{2,1,0:T(8,128)} %bitcast.18), custom_call_target="tpu_custom_call" | custom-call | tf_op jit(solution)/shard_map/exchange/pallas_call | solution.py:481
  114.9 4.8 %place.1 = bf16[320,2,16,128]{3,2,1,0:T(8,128)(2,1)} custom-call(s32[8,384]{1,0:T(8,128)} %tables.1.tab, bf16[4,4,64,16,128]{4,3,2,1,0:T(8,128)(2,1)} %get-tuple-element.7.ag, f32[4,8,128]{2,1,0:T(8,128)} %get-tuple-element.8.sq), custom_call_target="tpu_custom_call" | custom-call | tf_op jit(solution)/shard_map/place/pallas_call | solution.py:509
